TPU v7x, 256 devices: a whole 4x4x8 slice. The times are simulated.
256 devices in a mesh: frame: 128 (over y, x, z), tensor: 2 (over core).
Axes of the slice: x: 4, y: 4, z: 8, core: 2. Of those that a mesh axis runs over, the one named last changes fastest.
Arguments:
- queries: bfloat16 [65536, 3072], P('frame', 'tensor'), may hold values from -128 to 128
- context_keys: bfloat16 [1152, 3072], P(None, 'tensor'), may hold values from -8 to 8
- context_values: bfloat16 [1152, 3072], P(None, 'tensor'), may hold values from -6 to 6
- router_logit: float32 [65536], P('frame'), may hold values from -8 to 8
- keep_index: int32 [128, 512], P('frame'), may hold values from 0 to 512, as said below
- visible_blocks: int32 [128], P('frame'), may hold values from 1 to 9, as said below
- out_grad: bfloat16 [65536, 3072], P('frame', 'tensor'), may hold values from -12 to 12
Outputs:
- routed_out: bfloat16 [65536, 3072], P('frame', 'tensor')
- query_grad: bfloat16 [65536, 3072], P('frame', 'tensor')
- router_grad: float32 [65536], P('frame')
Inputs may be any that keep to these rules, and one draw needn't show every extreme that they name: `keep_index`: row f lists the tokens of frame f that the routed layer keeps, in rising order, then 512 in every unused place. All rows together keep exactly 16384 tokens, every frame keeps at least one, and one frame keeps all 512. The tokens of frame f see the context rows of memory blocks 0 to visible_blocks[f] - 1, blocks of 128 rows. It never falls from one frame to the next; the first frame sees one block and the last all 9.
All inputs are finite; a program needn't handle non-finite values.
Results may differ from a plain program's by a relative error of at most 0.0064.
Values may be sent and summed in bfloat16 or wider, within the bound.
A program may use at most 128 MiB of HBM per device.

v0:
```python
import functools

import jax
import jax.numpy as jnp
from jax import lax
from jax.experimental import pallas as pl
from jax.experimental.pallas import tpu as pltpu
from jax.sharding import PartitionSpec as P

HD = 128
MEM_BLOCK = 128
SCALE = HD ** (-0.5)
LOG2E = 1.4426950408889634
PAIR = 2
ROWS = 128

NT = (((1,), (1,)), ((), ()))


def dot(a, b):
    return jnp.dot(a, b, preferred_element_type=jnp.float32)


def dot_nt(a, b):
    return lax.dot_general(a, b, NT, preferred_element_type=jnp.float32)


def attend(q, g, keys, values):
    scores = dot_nt(q, keys)
    top = jnp.max(scores, axis=1, keepdims=True)
    terms = jnp.exp2((scores - top) * (SCALE * LOG2E))
    ones = jnp.ones(values.shape, values.dtype)
    sums = dot(terms.astype(jnp.bfloat16), jnp.concatenate([values, ones], axis=1))
    inverse = 1.0 / sums[:, HD:]
    mixed = sums[:, :HD] * inverse
    delta = jnp.sum(g.astype(jnp.float32) * mixed, axis=1, keepdims=True)
    dprob = dot_nt(g, values)
    dscore = (terms * (dprob - delta)).astype(jnp.bfloat16)
    dq = dot(dscore, keys) * (inverse * SCALE)
    return mixed.astype(jnp.bfloat16), dq.astype(jnp.bfloat16)


def kernel(
    visible_ref, keep_ref, logit_ref, q_ref, k_ref, v_ref, og_ref,
    out_ref, dq_ref, part_ref,
    gate, pick, place, qc, gc, ac, dc, acc, count_ref,
):
    tokens = q_ref.shape[0]
    blocks = k_ref.shape[0] // MEM_BLOCK
    step = pl.program_id(0)

    @pl.when(step == 0)
    def _():
        keep = keep_ref[...]
        count_ref[0] = jnp.sum((keep < tokens).astype(jnp.int32))
        spread = jnp.broadcast_to(logit_ref[...], (HD, tokens))
        gate[...] = jax.nn.sigmoid(jnp.transpose(spread))
        acc[...] = jnp.zeros_like(acc)
        token = lax.broadcasted_iota(jnp.int32, (tokens, tokens), 0)
        onehot = jnp.where(token == keep, 1.0, 0.0)
        place[...] = onehot.astype(jnp.bfloat16)
        pick[...] = jnp.transpose(onehot).astype(jnp.bfloat16)
        ac[...] = jnp.zeros_like(ac)
        dc[...] = jnp.zeros_like(dc)

    count = count_ref[0]
    full = count == tokens
    g_all = gate[...]
    gated = jnp.concatenate(
        [
            (g_all * og_ref[:, h * HD : (h + 1) * HD].astype(jnp.float32)).astype(jnp.bfloat16)
            for h in range(PAIR)
        ],
        axis=1,
    )

    @pl.when(full)
    def _():
        qc[...] = q_ref[...]
        gc[...] = gated

    @pl.when(jnp.logical_not(full))
    def _():
        qc[...] = dot(pick[...], q_ref[...]).astype(jnp.bfloat16)
        gc[...] = dot(pick[...], gated).astype(jnp.bfloat16)

    tiles = (count + (ROWS - 1)) // ROWS
    visible = visible_ref[0]
    for reach in range(1, blocks + 1):

        @pl.when(visible == reach)
        def _():
            span = reach * MEM_BLOCK

            @pl.loop(0, tiles)
            def _(tile):
                rows = pl.ds(pl.multiple_of(tile * ROWS, ROWS), ROWS)
                for h in range(PAIR):
                    cols = slice(h * HD, (h + 1) * HD)
                    mixed, dq = attend(
                        qc[rows, cols], gc[rows, cols], k_ref[:span, cols], v_ref[:span, cols]
                    )
                    ac[rows, cols] = mixed
                    dc[rows, cols] = dq

    def finish(attn):
        total = acc[...]
        for h in range(PAIR):
            cols = slice(h * HD, (h + 1) * HD)
            part = attn[:, cols].astype(jnp.float32)
            out_ref[:, cols] = (g_all * part).astype(jnp.bfloat16)
            total = total + og_ref[:, cols].astype(jnp.float32) * part
        acc[...] = total

    @pl.when(full)
    def _():
        finish(ac[...])
        dq_ref[...] = dc[...]

    @pl.when(jnp.logical_not(full))
    def _():
        finish(dot(place[...], ac[...]).astype(jnp.bfloat16))
        dq_ref[...] = dot(place[...], dc[...]).astype(jnp.bfloat16)

    @pl.when(step == pl.num_programs(0) - 1)
    def _():
        turned = jnp.transpose(acc[...])
        gated_row = jax.nn.sigmoid(logit_ref[...])
        part_ref[...] = jnp.sum(turned, axis=0, keepdims=True) * (gated_row * (1.0 - gated_row))


def local(queries, keys, values, logit, keep, visible, out_grad):
    tokens, width = queries.shape
    ctx = keys.shape[0]
    wide = PAIR * HD
    column = lambda rows: pl.BlockSpec((rows, wide), lambda s: (0, s))
    whole = pl.BlockSpec((1, tokens), lambda s: (0, 0))
    return pl.pallas_call(
        kernel,
        grid=(width // wide,),
        in_specs=[
            pl.BlockSpec(memory_space=pltpu.SMEM),
            whole,
            whole,
            column(tokens),
            column(ctx),
            column(ctx),
            column(tokens),
        ],
        out_specs=[column(tokens), column(tokens), whole],
        out_shape=[
            jax.ShapeDtypeStruct((tokens, width), jnp.bfloat16),
            jax.ShapeDtypeStruct((tokens, width), jnp.bfloat16),
            jax.ShapeDtypeStruct((1, tokens), jnp.float32),
        ],
        scratch_shapes=[
            pltpu.VMEM((tokens, HD), jnp.float32),
            pltpu.VMEM((tokens, tokens), jnp.bfloat16),
            pltpu.VMEM((tokens, tokens), jnp.bfloat16),
            pltpu.VMEM((tokens, wide), jnp.bfloat16),
            pltpu.VMEM((tokens, wide), jnp.bfloat16),
            pltpu.VMEM((tokens, wide), jnp.bfloat16),
            pltpu.VMEM((tokens, wide), jnp.bfloat16),
            pltpu.VMEM((tokens, HD), jnp.float32),
            pltpu.SMEM((1,), jnp.int32),
        ],
        compiler_params=pltpu.CompilerParams(
            dimension_semantics=("arbitrary",), vmem_limit_bytes=48 * 1024 * 1024
        ),
    )(visible, keep, logit.reshape(1, tokens), queries, keys, values, out_grad)


def per_device(queries, context_keys, context_values, router_logit, keep_index, visible_blocks, out_grad):
    routed_out, query_grad, part = local(
        queries, context_keys, context_values, router_logit, keep_index, visible_blocks, out_grad
    )
    router_grad = lax.psum(part.reshape(-1), "tensor")
    return routed_out, query_grad, router_grad


def solution(mesh):
    return jax.shard_map(
        per_device,
        mesh=mesh,
        in_specs=(
            P("frame", "tensor"),
            P(None, "tensor"),
            P(None, "tensor"),
            P("frame"),
            P("frame", None),
            P("frame"),
            P("frame", "tensor"),
        ),
        out_specs=(P("frame", "tensor"), P("frame", "tensor"), P("frame")),
        check_vma=False,
    )
```

profile of v0, /device:TPU:155, one launch (start us, length us, event | category | flops | bytes accessed | tf_op | source)
XLA Modules:
  0.0 48.9 jit_solution(13049183553071735228)
XLA Ops:
  1.3 0.0 copy-start
  1.3 1.4 %copy-done = bf16[512,1536]{1,0:T(8,128)(2,1)S(1)} copy-done((bf16[512,1536]{1,0:T(8,128)(2,1)S(1)}, bf16[512,1536]{1,0:T(8,128)(2,1)}, u32[]{:S(2)}) %copy-start) | copy-done | bytes 1572888
  2.7 0.0 copy-start.1
  2.7 1.4 %copy-done.1 = bf16[512,1536]{1,0:T(8,128)(2,1)S(1)} copy-done((bf16[512,1536]{1,0:T(8,128)(2,1)S(1)}, bf16[512,1536]{1,0:T(8,128)(2,1)}, u32[]{:S(2)}) %copy-start.1) | copy-done | bytes 1572888
  4.1 0.0 copy-start.2
  4.1 0.7 %copy-done.2 = s32[1,512]{1,0:T(1,128)S(1)} copy-done((s32[1,512]{1,0:T(1,128)S(1)}, s32[1,512]{1,0:T(1,128)}, u32[]{:S(2)}) %copy-start.2) | copy-done | bytes 2072
  4.8 0.0 copy-start.3
  4.8 0.7 %copy-done.3 = f32[512]{0:T(512)S(1)} copy-done((f32[512]{0:T(512)S(1)}, f32[512]{0:T(512)}, u32[]{:S(2)}) %copy-start.3) | copy-done | bytes 2072
  5.5 40.1 %shard_map.94 = (bf16[512,1536]{1,0:T(8,128)(2,1)}, bf16[512,1536]{1,0:T(8,128)(2,1)}, f32[1,512]{1,0:T(1,128)S(1)}) custom-call(s32[1]{0:T(128)S(6)} %copy.10.visible_ref, s32[1,512]{1,0:T(1,128)S(1)} %copy-done.2, f32[1,512]{1,0:T(1,128)S(1)} %bitcast.2, bf16[512,1536]{1,0:T(8,128)(2,1)S(1)} %copy-done, bf16[1152,1536]{1,0:T(8,128)(2,1)} %k_ref.1, ...), custom_call_target="tpu_custom_call" | custom-call | tf_op jit(solution)/shard_map/pallas_call | solution.py:138
  45.5 3.4 %psum.7 = f32[512]{0:T(512)} all-reduce(f32[512]{0:T(512)S(1)} %bitcast.3), channel_id=1, replica_groups=mesh['frame'=128,'tensor'=2] {'tensor'}, use_global_device_ids=true, to_apply=%region_0.0 | all-reduce | flops 512 | bytes 4096 | tf_op jit(solution)/shard_map/psum | solution.py:177
Async XLA Ops:
  1.3 1.4 %copy-start = (bf16[512,1536]{1,0:T(8,128)(2,1)S(1)}, bf16[512,1536]{1,0:T(8,128)(2,1)}, u32[]{:S(2)}) copy-start(bf16[512,1536]{1,0:T(8,128)(2,1)} %q_ref.1) | copy-start | bytes 4718596
  2.7 1.4 %copy-start.1 = (bf16[512,1536]{1,0:T(8,128)(2,1)S(1)}, bf16[512,1536]{1,0:T(8,128)(2,1)}, u32[]{:S(2)}) copy-start(bf16[512,1536]{1,0:T(8,128)(2,1)} %og_ref.1) | copy-start | bytes 4718596
  4.1 0.7 %copy-start.2 = (s32[1,512]{1,0:T(1,128)S(1)}, s32[1,512]{1,0:T(1,128)}, u32[]{:S(2)}) copy-start(s32[1,512]{1,0:T(1,128)} %keep_ref.1) | copy-start | bytes 6148
  4.8 0.7 %copy-start.3 = (f32[512]{0:T(512)S(1)}, f32[512]{0:T(512)}, u32[]{:S(2)}) copy-start(f32[512]{0:T(512)} %param.10) | copy-start | bytes 6148
where the time goes:
time: 49.1 us; the launch traced here: 48.9 us
  Pallas kernels  40.1 us (82%)
  local copies, waits for them, and re-layouts  4.17 us (8%)
  blocking collectives  3.36 us (7%)
  between operations  1.29 us (3%)
    pallas_call x1, Pallas kernels, local(): pl.pallas_call(kernel, grid=(width // wide,), in_specs=[pl.BlockSpec(memo...  40.1 us
    unnamed x8, local copies, waits for them, and re-layouts  4.17 us
    psum x1, blocking collectives, per_device(): router_grad = lax.psum(part.reshape(-1), 'tensor')  3.36 us

commit v1 on v0

v1 whole, which is shorter than its diff:
```python
import jax
import jax.numpy as jnp
from jax import lax
from jax.experimental import pallas as pl
from jax.experimental.pallas import tpu as pltpu
from jax.sharding import PartitionSpec as P

HD = 128
MEM_BLOCK = 128
SCALE = HD ** (-0.5)
LOG2E = 1.4426950408889634
UNIT = 2
FEW_UNITS = 2
ROWS = 256
FEW = 224
AHEAD = 2
MANY_REACH = (4, 5, 6, 7, 8, 9)
FEW_REACH = (8, 9)


def dot(a, b):
    return jnp.dot(a, b, preferred_element_type=jnp.float32)


def dot_nt(a, b):
    return lax.dot_general(a, b, (((1,), (1,)), ((), ())), preferred_element_type=jnp.float32)


def half(a):
    return a.astype(jnp.bfloat16)


def attend(q, g, keys, values, hidden):
    heads = range(len(q))
    scores = [dot_nt(q[h], keys[h]) for h in heads]
    dprob = [dot_nt(g[h], values[h]) for h in heads]
    if hidden is not None:
        scores = [hidden(s) for s in scores]
    top = [jnp.max(scores[h], axis=1, keepdims=True) for h in heads]
    terms = [jnp.exp2((scores[h] - top[h]) * (SCALE * LOG2E)) for h in heads]
    ones = jnp.ones(values[0].shape, values[0].dtype)
    sums = [dot(half(terms[h]), jnp.concatenate([values[h], ones], axis=1)) for h in heads]
    inverse = [1.0 / sums[h][:, HD:] for h in heads]
    mixed = [sums[h][:, :HD] * inverse[h] for h in heads]
    delta = [jnp.sum(g[h].astype(jnp.float32) * mixed[h], axis=1, keepdims=True) for h in heads]
    dscore = [half(terms[h] * (dprob[h] - delta[h])) for h in heads]
    dq = [dot(dscore[h], keys[h]) * (inverse[h] * SCALE) for h in heads]
    return [half(m).astype(jnp.float32) for m in mixed], [half(d) for d in dq]


def kernel(
    visible_hbm, keep_hbm, logit_hbm, q_hbm, k_hbm, v_hbm, og_hbm,
    out_hbm, dq_hbm, part_hbm,
    visible, keep_scalar, keep, logit, q_all, k_all, v_all, og_all, out_all, dq_all, part,
    gate, pick, place, acc, small_sem, in_sem, out_sem,
):
    tokens, width = q_all.shape
    unit = UNIT * HD
    groups = width // unit

    def columns(group, units=1):
        return pl.ds(pl.multiple_of(group * unit, unit), units * unit)

    def loads(group):
        cols = columns(group)
        pairs = ((q_hbm, q_all), (k_hbm, k_all), (og_hbm, og_all), (v_hbm, v_all))
        return [
            pltpu.make_async_copy(src.at[:, cols], dst.at[:, cols], in_sem.at[i, group])
            for i, (src, dst) in enumerate(pairs)
        ]

    def stores(group):
        cols = columns(group)
        pairs = ((out_all, out_hbm), (dq_all, dq_hbm))
        return [
            pltpu.make_async_copy(src.at[:, cols], dst.at[:, cols], out_sem.at[i, group])
            for i, (src, dst) in enumerate(pairs)
        ]

    small = [
        pltpu.make_async_copy(src, dst, small_sem.at[i])
        for i, (src, dst) in enumerate(
            ((visible_hbm, visible), (keep_hbm, keep_scalar), (keep_hbm, keep), (logit_hbm, logit))
        )
    ]
    for copy in small:
        copy.start()
    for group in range(AHEAD):
        for copy in loads(group):
            copy.start()
    for copy in small:
        copy.wait()

    gate_row = jax.nn.sigmoid(logit[...])
    gate[...] = jnp.transpose(jnp.broadcast_to(gate_row, (HD, tokens)))
    acc[...] = jnp.zeros_like(acc)
    shown = visible[0]
    full = keep_scalar[0, tokens - 1] < tokens
    few = keep_scalar[0, FEW] >= tokens
    some = jnp.logical_not(full)
    many = jnp.logical_not(few)

    @pl.when(some)
    def _():
        kept = keep[...]
        token = lax.broadcasted_iota(jnp.int32, (tokens, tokens), 0)
        place[...] = half(jnp.where(token == kept, 1.0, 0.0))
        spread = jnp.transpose(jnp.broadcast_to(kept.astype(jnp.float32), (HD, tokens)))
        lane = lax.broadcasted_iota(jnp.int32, (tokens, HD), 1).astype(jnp.float32)
        own = jnp.zeros((tokens, HD), jnp.float32)
        for start in range(0, tokens, HD):
            hit = jnp.where(spread == lane + float(start), 1.0, 0.0)
            pick[:, start : start + HD] = half(hit)
            own = own + hit * gate_row[:, start : start + HD]
        gate[...] = jnp.broadcast_to(jnp.sum(own, axis=1, keepdims=True), (tokens, HD))

    def sweep(units, body):
        @pl.loop(0, groups // units)
        def _(index):
            first = index * units
            for part_of in range(units):
                for copy in loads(first + part_of):
                    copy.wait()

            @pl.when(first + AHEAD < groups)
            def _():
                for part_of in range(units):
                    for copy in loads(first + AHEAD + part_of):
                        copy.start()

            body(first)
            for part_of in range(units):
                for copy in stores(first + part_of):
                    copy.start()

    def head_columns(group, units=1):
        return [
            pl.ds(pl.multiple_of(group * unit + h * HD, HD), HD) for h in range(units * UNIT)
        ]

    def hide(span, exact):
        if exact:
            return None

        def hidden(scores):
            col = lax.broadcasted_iota(jnp.int32, scores.shape, 1)
            return jnp.where(col < shown * MEM_BLOCK, scores, -jnp.inf)

        return hidden

    def tile(span, exact, cols, q, og, gates):
        g = [half(gates * o) for o in og]
        attn, dq = attend(
            q, g, [k_all[:span, c] for c in cols], [v_all[:span, c] for c in cols], hide(span, exact)
        )
        inner = og[0] * attn[0]
        for o, a in zip(og[1:], attn[1:]):
            inner = inner + o * a
        return [half(gates * a) for a in attn], dq, inner

    def run_many(span, exact, group):
        wide_cols = columns(group)
        cols = head_columns(group)

        @pl.when(some)
        def _():
            q_all[:, wide_cols] = half(dot(pick[...], q_all[:, wide_cols]))
            og_all[:, wide_cols] = half(dot(pick[...], og_all[:, wide_cols]))

        routed, dq, inner = tile(
            span, exact, cols,
            [q_all[:, c] for c in cols],
            [og_all[:, c].astype(jnp.float32) for c in cols],
            gate[...],
        )
        for h, c in enumerate(cols):
            out_all[:, c] = routed[h]
            dq_all[:, c] = dq[h]
        acc[...] = acc[...] + inner

        @pl.when(some)
        def _():
            out_all[:, wide_cols] = half(dot(place[...], out_all[:, wide_cols]))
            dq_all[:, wide_cols] = half(dot(place[...], dq_all[:, wide_cols]))

    def run_few(span, exact, group):
        wide_cols = columns(group, FEW_UNITS)
        cols = head_columns(group, FEW_UNITS)
        chosen = pick[:FEW, :]
        q = half(dot(chosen, q_all[:, wide_cols]))
        og = dot(chosen, og_all[:, wide_cols])
        routed, dq, inner = tile(
            span, exact, cols,
            [q[:, h * HD : (h + 1) * HD] for h in range(len(cols))],
            [og[:, h * HD : (h + 1) * HD] for h in range(len(cols))],
            gate[:FEW, :],
        )
        acc[:FEW, :] = acc[:FEW, :] + inner
        blank = jnp.zeros((ROWS - FEW, FEW_UNITS * unit), jnp.bfloat16)
        for target, rows in ((out_all, routed), (dq_all, dq)):
            stacked = jnp.concatenate([jnp.concatenate(rows, axis=1), blank], axis=0)
            target[:, wide_cols] = half(dot(place[:, :ROWS], stacked))

    def choose(reaches, run, wanted, units):
        low = 0
        for reach in reaches:
            span, exact = reach * MEM_BLOCK, reach == low + 1
            here = jnp.logical_and(shown > low, shown <= reach)

            @pl.when(jnp.logical_and(here, wanted))
            def _():
                sweep(units, lambda group: run(span, exact, group))

            low = reach

    choose(FEW_REACH, run_few, few, FEW_UNITS)
    choose(MANY_REACH, run_many, many, 1)

    weight = gate_row * (1.0 - gate_row)

    @pl.when(full)
    def _():
        part[...] = jnp.sum(jnp.transpose(acc[...]), axis=0, keepdims=True) * weight

    @pl.when(some)
    def _():
        inner = jnp.sum(acc[...], axis=1, keepdims=True)
        part[...] = jnp.sum(pick[...].astype(jnp.float32) * inner, axis=0, keepdims=True) * weight

    last = pltpu.make_async_copy(part, part_hbm, small_sem.at[0])
    last.start()
    for group in range(groups):
        for copy in stores(group):
            copy.wait()
    last.wait()


def local(queries, keys, values, logit, keep, visible, out_grad):
    tokens, width = queries.shape
    ctx = keys.shape[0]
    groups = width // (UNIT * HD)
    hbm = pl.BlockSpec(memory_space=pl.ANY)
    return pl.pallas_call(
        kernel,
        in_specs=[hbm] * 7,
        out_specs=[hbm] * 3,
        out_shape=[
            jax.ShapeDtypeStruct((tokens, width), jnp.bfloat16),
            jax.ShapeDtypeStruct((tokens, width), jnp.bfloat16),
            jax.ShapeDtypeStruct((1, tokens), jnp.float32),
        ],
        scratch_shapes=[
            pltpu.SMEM((1,), jnp.int32),
            pltpu.SMEM((1, tokens), jnp.int32),
            pltpu.VMEM((1, tokens), jnp.int32),
            pltpu.VMEM((1, tokens), jnp.float32),
            pltpu.VMEM((tokens, width), jnp.bfloat16),
            pltpu.VMEM((ctx, width), jnp.bfloat16),
            pltpu.VMEM((ctx, width), jnp.bfloat16),
            pltpu.VMEM((tokens, width), jnp.bfloat16),
            pltpu.VMEM((tokens, width), jnp.bfloat16),
            pltpu.VMEM((tokens, width), jnp.bfloat16),
            pltpu.VMEM((1, tokens), jnp.float32),
            pltpu.VMEM((tokens, HD), jnp.float32),
            pltpu.VMEM((tokens, tokens), jnp.bfloat16),
            pltpu.VMEM((tokens, tokens), jnp.bfloat16),
            pltpu.VMEM((tokens, HD), jnp.float32),
            pltpu.SemaphoreType.DMA((4,)),
            pltpu.SemaphoreType.DMA((4, groups)),
            pltpu.SemaphoreType.DMA((2, groups)),
        ],
        compiler_params=pltpu.CompilerParams(vmem_limit_bytes=60 * 1024 * 1024),
    )(visible, keep, logit.reshape(1, tokens), queries, keys, values, out_grad)


def per_device(queries, context_keys, context_values, router_logit, keep_index, visible_blocks, out_grad):
    routed_out, query_grad, part = local(
        queries, context_keys, context_values, router_logit, keep_index, visible_blocks, out_grad
    )
    router_grad = lax.psum(part.reshape(-1), "tensor")
    return routed_out, query_grad, router_grad


def solution(mesh):
    return jax.shard_map(
        per_device,
        mesh=mesh,
        in_specs=(
            P("frame", "tensor"),
            P(None, "tensor"),
            P(None, "tensor"),
            P("frame"),
            P("frame", None),
            P("frame"),
            P("frame", "tensor"),
        ),
        out_specs=(P("frame", "tensor"), P("frame", "tensor"), P("frame")),
        check_vma=False,
    )
```

time: 49.1 us -> 21.1 us (0.43)
  the two profiles are of different devices: /device:TPU:155 before, /device:TPU:1 now
where the time goes in v1:
time: 21.1 us; the launch traced here: 21 us
  Pallas kernels  13.7 us (65%)
  blocking collectives  6.07 us (29%)
  between operations  1.29 us (6%)
    pallas_call x1, Pallas kernels, local(): pl.pallas_call(kernel, in_specs=[hbm] * 7, out_specs=[hbm] * 3, out_shape...  13.7 us
    psum x1, blocking collectives, per_device(): router_grad = lax.psum(part.reshape(-1), 'tensor')  6.07 us

profile of v1, /device:TPU:1, one launch (start us, length us, event | category | flops | bytes accessed | tf_op | source)
XLA Modules:
  0.0 21.0 jit_solution(1807622989025874767)
XLA Ops:
  1.3 13.7 %shard_map.94 = (bf16[512,1536]{1,0:T(8,128)(2,1)}, bf16[512,1536]{1,0:T(8,128)(2,1)}, f32[1,512]{1,0:T(1,128)}) custom-call(s32[1]{0:T(128)S(6)} %copy.10.visible_hbm, s32[1,512]{1,0:T(1,128)} %keep_hbm.1, f32[1,512]{1,0:T(1,128)} %bitcast.2, bf16[512,1536]{1,0:T(8,128)(2,1)} %q_hbm.1, bf16[1152,1536]{1,0:T(8,128)(2,1)} %k_hbm.1, bf16[1152,1536]{1,0:T(8,128)(2,1)} %v_hbm.1, ...), custom_call_target="tpu_custom_call" | custom-call | tf_op jit(solution)/shard_map/pallas_call | solution.py:243
  14.9 6.1 %psum.7 = f32[512]{0:T(512)} all-reduce(f32[512]{0:T(512)} %bitcast.3), channel_id=1, replica_groups=mesh['frame'=128,'tensor'=2] {'tensor'}, use_global_device_ids=true, to_apply=%region_0.0 | all-reduce | flops 512 | bytes 4096 | tf_op jit(solution)/shard_map/psum | solution.py:280

commit v2 on v1

--- a/solution.py
+++ b/solution.py
@@ -15,7 +15,7 @@
 FEW = 224
 AHEAD = 2
 MANY_REACH = (4, 5, 6, 7, 8, 9)
-FEW_REACH = (8, 9)
+FEW_REACH = (2, 8, 9)
 
 
 def dot(a, b):
@@ -201,20 +201,23 @@
             stacked = jnp.concatenate([jnp.concatenate(rows, axis=1), blank], axis=0)
             target[:, wide_cols] = half(dot(place[:, :ROWS], stacked))
 
-    def choose(reaches, run, wanted, units):
-        low = 0
-        for reach in reaches:
-            span, exact = reach * MEM_BLOCK, reach == low + 1
-            here = jnp.logical_and(shown > low, shown <= reach)
-
-            @pl.when(jnp.logical_and(here, wanted))
-            def _():
-                sweep(units, lambda group: run(span, exact, group))
-
-            low = reach
-
-    choose(FEW_REACH, run_few, few, FEW_UNITS)
-    choose(MANY_REACH, run_many, many, 1)
+    def choose(reaches, run, units):
+        reach, low = reaches[-1], (0, *reaches)[-2]
+        span, exact = reach * MEM_BLOCK, reach == low + 1
+
+        def here():
+            sweep(units, lambda group: run(span, exact, group))
+
+        if low:
+            lax.cond(shown > low, here, lambda: choose(reaches[:-1], run, units))
+        else:
+            here()
+
+    lax.cond(
+        few,
+        lambda: choose(FEW_REACH, run_few, FEW_UNITS),
+        lambda: choose(MANY_REACH, run_many, 1),
+    )
 
     weight = gate_row * (1.0 - gate_row)
 

time: 21.1 us -> 20.6 us (0.976)
  the two profiles are of different devices: /device:TPU:1 before, /device:TPU:207 now
where the time goes in v2:
time: 20.6 us; the launch traced here: 20.4 us
  Pallas kernels  15.6 us (76%)
  blocking collectives  3.5 us (17%)
  between operations  1.29 us (6%)
    pallas_call x1, Pallas kernels, local(): pl.pallas_call(kernel, in_specs=[hbm] * 7, out_specs=[hbm] * 3, out_shape...  15.6 us
    psum x1, blocking collectives, per_device(): router_grad = lax.psum(part.reshape(-1), 'tensor')  3.5 us

profile of v2, /device:TPU:207, one launch (start us, length us, event | category | flops | bytes accessed | tf_op | source)
XLA Modules:
  0.0 20.4 jit_solution(868906701728499010)
XLA Ops:
  1.3 15.6 %shard_map.94 = (bf16[512,1536]{1,0:T(8,128)(2,1)}, bf16[512,1536]{1,0:T(8,128)(2,1)}, f32[1,512]{1,0:T(1,128)}) custom-call(s32[1]{0:T(128)S(6)} %copy.10.visible_hbm, s32[1,512]{1,0:T(1,128)} %keep_hbm.1, f32[1,512]{1,0:T(1,128)} %bitcast.2, bf16[512,1536]{1,0:T(8,128)(2,1)} %q_hbm.1, bf16[1152,1536]{1,0:T(8,128)(2,1)} %k_hbm.1, bf16[1152,1536]{1,0:T(8,128)(2,1)} %v_hbm.1, ...), custom_call_target="tpu_custom_call" | custom-call | tf_op jit(solution)/shard_map/pallas_call | solution.py:246
  16.9 3.5 %psum.7 = f32[512]{0:T(512)} all-reduce(f32[512]{0:T(512)} %bitcast.3), channel_id=1, replica_groups=mesh['frame'=128,'tensor'=2] {'tensor'}, use_global_device_ids=true, to_apply=%region_0.0 | all-reduce | flops 512 | bytes 4096 | tf_op jit(solution)/shard_map/psum | solution.py:283

commit v3 on v2

--- a/solution.py
+++ b/solution.py
@@ -49,9 +49,9 @@
 
 
 def kernel(
-    visible_hbm, keep_hbm, logit_hbm, q_hbm, k_hbm, v_hbm, og_hbm,
-    out_hbm, dq_hbm, part_hbm,
-    visible, keep_scalar, keep, logit, q_all, k_all, v_all, og_all, out_all, dq_all, part,
+    visible, keep_hbm, logit_hbm, q_hbm, k_hbm, v_hbm, og_hbm,
+    out_hbm, dq_hbm, part,
+    keep_scalar, keep, logit, q_all, k_all, v_all, og_all, out_all, dq_all,
     gate, pick, place, acc, small_sem, in_sem, out_sem,
 ):
     tokens, width = q_all.shape
@@ -80,7 +80,7 @@
     small = [
         pltpu.make_async_copy(src, dst, small_sem.at[i])
         for i, (src, dst) in enumerate(
-            ((visible_hbm, visible), (keep_hbm, keep_scalar), (keep_hbm, keep), (logit_hbm, logit))
+            ((keep_hbm, keep_scalar), (keep_hbm, keep), (logit_hbm, logit))
         )
     ]
     for copy in small:
@@ -230,30 +230,26 @@
         inner = jnp.sum(acc[...], axis=1, keepdims=True)
         part[...] = jnp.sum(pick[...].astype(jnp.float32) * inner, axis=0, keepdims=True) * weight
 
-    last = pltpu.make_async_copy(part, part_hbm, small_sem.at[0])
-    last.start()
     for group in range(groups):
         for copy in stores(group):
             copy.wait()
-    last.wait()
 
 
 def local(queries, keys, values, logit, keep, visible, out_grad):
     tokens, width = queries.shape
     ctx = keys.shape[0]
     groups = width // (UNIT * HD)
-    hbm = pl.BlockSpec(memory_space=pl.ANY)
+    hbm = pl.BlockSpec(memory_space=pltpu.HBM)
     return pl.pallas_call(
         kernel,
-        in_specs=[hbm] * 7,
-        out_specs=[hbm] * 3,
+        in_specs=[pl.BlockSpec(memory_space=pltpu.SMEM)] + [hbm] * 6,
+        out_specs=[hbm, hbm, pl.BlockSpec(memory_space=pltpu.VMEM)],
         out_shape=[
             jax.ShapeDtypeStruct((tokens, width), jnp.bfloat16),
             jax.ShapeDtypeStruct((tokens, width), jnp.bfloat16),
-            jax.ShapeDtypeStruct((1, tokens), jnp.float32),
+            pltpu.VMEM((1, tokens), jnp.float32),
         ],
         scratch_shapes=[
-            pltpu.SMEM((1,), jnp.int32),
             pltpu.SMEM((1, tokens), jnp.int32),
             pltpu.VMEM((1, tokens), jnp.int32),
             pltpu.VMEM((1, tokens), jnp.float32),
@@ -263,12 +259,11 @@
             pltpu.VMEM((tokens, width), jnp.bfloat16),
             pltpu.VMEM((tokens, width), jnp.bfloat16),
             pltpu.VMEM((tokens, width), jnp.bfloat16),
-            pltpu.VMEM((1, tokens), jnp.float32),
             pltpu.VMEM((tokens, HD), jnp.float32),
             pltpu.VMEM((tokens, tokens), jnp.bfloat16),
             pltpu.VMEM((tokens, tokens), jnp.bfloat16),
             pltpu.VMEM((tokens, HD), jnp.float32),
-            pltpu.SemaphoreType.DMA((4,)),
+            pltpu.SemaphoreType.DMA((3,)),
             pltpu.SemaphoreType.DMA((4, groups)),
             pltpu.SemaphoreType.DMA((2, groups)),
         ],
@@ -276,12 +271,40 @@
     )(visible, keep, logit.reshape(1, tokens), queries, keys, values, out_grad)
 
 
+def exchange(mine, total, theirs, send, recv):
+    peer = {"tensor": 1 - lax.axis_index("tensor")}
+    barrier = pltpu.get_barrier_semaphore()
+    pl.semaphore_signal(barrier, inc=1, device_id=peer, device_id_type=pl.DeviceIdType.MESH)
+    pl.semaphore_wait(barrier, 1)
+    copy = pltpu.make_async_remote_copy(
+        mine, theirs, send, recv, device_id=peer, device_id_type=pl.DeviceIdType.MESH
+    )
+    copy.start()
+    copy.wait()
+    total[...] = mine[...] + theirs[...]
+
+
+def add_cores(part):
+    vmem = pl.BlockSpec(memory_space=pltpu.VMEM)
+    return pl.pallas_call(
+        exchange,
+        in_specs=[vmem],
+        out_specs=vmem,
+        out_shape=pltpu.VMEM(part.shape, part.dtype),
+        scratch_shapes=[
+            pltpu.VMEM(part.shape, part.dtype),
+            pltpu.SemaphoreType.DMA,
+            pltpu.SemaphoreType.DMA,
+        ],
+        compiler_params=pltpu.CompilerParams(collective_id=0, has_side_effects=True),
+    )(pltpu.with_memory_space_constraint(part, pltpu.VMEM))
+
+
 def per_device(queries, context_keys, context_values, router_logit, keep_index, visible_blocks, out_grad):
     routed_out, query_grad, part = local(
         queries, context_keys, context_values, router_logit, keep_index, visible_blocks, out_grad
     )
-    router_grad = lax.psum(part.reshape(-1), "tensor")
-    return routed_out, query_grad, router_grad
+    return routed_out, query_grad, add_cores(part).reshape(-1)
 
 
 def solution(mesh):

time: 20.6 us -> 17.6 us (0.85)
  the two profiles are of different devices: /device:TPU:207 before, /device:TPU:95 now
where the time goes in v3:
time: 17.6 us; the launch traced here: 17.5 us
  Pallas kernels  15.6 us (89%)
  between operations  1.29 us (7%)
  local copies, waits for them, and re-layouts  0.58 us (3%)
    pallas_call x1, Pallas kernels, local(): pl.pallas_call(kernel, in_specs=[pl.BlockSpec(memory_space=pltpu.SMEM)] +...  13.9 us
    pallas_call x1, Pallas kernels, add_cores(): pl.pallas_call(exchange, in_specs=[vmem], out_specs=vmem, out_shape=pltpu...  1.67 us
    unnamed x1, local copies, waits for them, and re-layouts  0.58 us

profile of v3, /device:TPU:95, one launch (start us, length us, event | category | flops | bytes accessed | tf_op | source)
XLA Modules:
  0.0 17.5 jit_solution(2565511935428097557)
XLA Ops:
  1.3 13.9 %shard_map.94 = (bf16[512,1536]{1,0:T(8,128)(2,1)}, bf16[512,1536]{1,0:T(8,128)(2,1)}, f32[1,512]{1,0:T(1,128)S(1)}) custom-call(s32[1]{0:T(128)S(6)} %copy.12.visible, s32[1,512]{1,0:T(1,128)} %keep_hbm.1, f32[1,512]{1,0:T(1,128)} %bitcast.3, bf16[512,1536]{1,0:T(8,128)(2,1)} %q_hbm.1, bf16[1152,1536]{1,0:T(8,128)(2,1)} %k_hbm.1, bf16[1152,1536]{1,0:T(8,128)(2,1)} %v_hbm.1, ...), custom_call_target="tpu_custom_call" | custom-call | tf_op jit(solution)/shard_map/pallas_call | solution.py:243
  15.2 1.7 %shard_map.95 = f32[1,512]{1,0:T(1,128)S(1)} custom-call(f32[1,512]{1,0:T(1,128)S(1)} %get-tuple-element.8.mine), custom_call_target="tpu_custom_call" | custom-call | tf_op jit(solution)/shard_map/pallas_call | solution.py:289
  16.9 0.6 %copy.11 = f32[512]{0:T(512)} copy(f32[512]{0:T(512)S(1)} %bitcast.2) | data formatting | bytes 4096
